TPU v7x, 128 devices: a whole 4x4x4 slice. The times are simulated.
128 devices in a mesh: dp: 4 (over x), expert: 32 (over z, y, core).
Axes of the slice: x: 4, y: 4, z: 4, core: 2. Of those that a mesh axis runs over, the one named last changes fastest.
Arguments:
- expert_ids: int32 [4, 4096, 2], P('dp', 'expert'), may hold values from 0 to 7, all different within a row; in each aligned block of 128 rows (0 to 127, 128 to 255, ..., all dimensions but the last counted through in order) at most 34 rows name the same one
- hidden_grad: bfloat16 [4352, 98304], P(None, ('dp', 'expert')), may hold values from -0.1796875 to 0.1796875
- up_weight: bfloat16 [4096, 98304], P(None, ('dp', 'expert')), may hold values from -2.390625 to 2.390625
Outputs:
- token_grad: bfloat16 [4, 4096, 4096], P('dp', 'expert')
Inputs may be any that keep to these rules, and one draw needn't show every extreme that they name: `expert_ids`: each token names 2 different experts; among the 128 tokens of one sequence shard no expert is named more than 34 times.
All inputs are finite; a program needn't handle non-finite values.
Results may differ from a plain program's by a relative error of at most 0.018.
Values may be sent and summed in bfloat16 or wider, within the bound.
A program may use at most 256 MiB of HBM per device.

v0:
```python
import jax
import jax.numpy as jnp
from jax import lax
from jax.sharding import PartitionSpec as P

EXPERTS = 8


def slot_positions(pair_ids, expert_count):
    flat_ids = pair_ids.reshape(-1)
    one_hot = (flat_ids[:, None] == jnp.arange(expert_count, dtype=jnp.int32)[None, :]).astype(
        jnp.int32
    )
    before = jnp.cumsum(one_hot, axis=0) - one_hot
    return jnp.sum(before * one_hot, axis=1).reshape(pair_ids.shape)


def on_device(expert_ids, hidden_grad, up_weight):
    groups = lax.axis_size("dp")
    columns = lax.axis_size("expert")
    split_count = columns // EXPERTS
    token_rows = expert_ids.shape[1]
    model_width = up_weight.shape[0]
    group_rows = hidden_grad.shape[0] // groups
    per_send = group_rows // columns
    local_ids = expert_ids[0]
    positions = slot_positions(local_ids, EXPERTS)
    slot_keys = local_ids * per_send + positions
    slot_range = jnp.arange(EXPERTS * per_send, dtype=jnp.int32)
    selector = jnp.any(slot_keys[None, :, :] == slot_range[:, None, None], axis=2).astype(
        jnp.bfloat16
    )
    summed = lax.psum_scatter(
        lax.dot_general(
            hidden_grad, up_weight, (((1,), (1,)), ((), ())), preferred_element_type=jnp.float32
        ).astype(jnp.bfloat16),
        "dp",
        scatter_dimension=0,
        tiled=True,
    )
    outgoing = summed.reshape(columns, per_send, model_width)
    returned = lax.all_to_all(outgoing, "expert", split_axis=0, concat_axis=0, tiled=True)
    returned = returned.reshape(EXPERTS, split_count, per_send, model_width)
    gathered_sum = jnp.zeros((token_rows, model_width), jnp.float32)
    for half_index in range(split_count):
        block_rows = returned[:, half_index].reshape(EXPERTS * per_send, model_width)
        gathered_sum = gathered_sum + lax.dot_general(
            selector, block_rows, (((0,), (0,)), ((), ())), preferred_element_type=jnp.float32
        )
    return gathered_sum.astype(jnp.bfloat16).reshape(1, token_rows, model_width)


def solution(mesh):
    return jax.shard_map(
        on_device,
        mesh=mesh,
        in_specs=(P("dp", "expert", None), P(None, ("dp", "expert")), P(None, ("dp", "expert"))),
        out_specs=P("dp", "expert", None),
        check_vma=False,
    )
```

profile of v0, /device:TPU:1, one launch (start us, length us, event | category | flops | bytes accessed | tf_op | source)
XLA Modules:
  0.0 521.0 jit_solution(13463437591599329598)
XLA Ops:
  6.5 0.0 reduce-scatter.4.cloned.1.call-start
  6.5 35.4 %convolution_convert_fusion = bf16[4352,4096]{1,0:T(8,128)(2,1)} fusion(bf16[4352,768]{1,0:T(8,128)(2,1)} %param.4, bf16[4096,768]{1,0:T(8,128)(2,1)} %param.5), kind=kOutput, calls=%fused_computation | convolution fusion | flops 27398242304 | bytes 48627712 | tf_op jit(solution)/shard_map/dot_general | solution.py:34
  42.0 0.0 reduce-scatter.4.cloned.1.call-update
  42.0 303.0 %reduce-scatter.4.cloned.1.call-done = bf16[1088,4096]{1,0:T(8,128)(2,1)} async-done(((bf16[4352,4096]{1,0:T(8,128)(2,1)}), bf16[1088,4096]{1,0:T(8,128)(2,1)}) %reduce-scatter.4.cloned.1.call-update) | async-done | bytes 8912912
  345.0 10.3 %reshape.32 = bf16[32,34,4096]{2,1,0:T(8,128)(2,1)} reshape(bf16[1088,4096]{1,0:T(8,128)(2,1)} %reduce-scatter.4.cloned.1.call-done) | data formatting | bytes 17825792 | tf_op jit(solution)/shard_map/reshape | solution.py:41
  355.3 0.0 copy-start.3
  355.3 7.8 %all-to-all-start = ((bf16[32,34,4096]{2,1,0:T(8,128)(2,1)}), bf16[32,34,4096]{2,1,0:T(8,128)(2,1)}, u32[]{:S(2)}, u32[]{:S(2)}) async-start(bf16[32,34,4096]{2,1,0:T(8,128)(2,1)} %reshape.32), calls=%async_computation | async-start | bytes 20971520 | tf_op jit(solution)/shard_map/all_to_all | solution.py:42
  363.2 0.0 copy-done.3
  363.2 0.1 copy.30
  363.3 0.1 eq.44
  363.4 0.1 eq.40
  363.6 0.6 reduce-window.6
  364.2 0.2 slice_reduce_fusion
  364.4 0.1 fusion.4
  364.5 0.1 reshape.31
  364.7 0.1 copy.32
  364.8 0.1 fusion.2
  364.8 123.6 %all-to-all-done = bf16[32,34,4096]{2,1,0:T(8,128)(2,1)} async-done(((bf16[32,34,4096]{2,1,0:T(8,128)(2,1)}), bf16[32,34,4096]{2,1,0:T(8,128)(2,1)}, u32[]{:S(2)}, u32[]{:S(2)}) %all-to-all-start) | async-done | bytes 8912928 | tf_op jit(solution)/shard_map/all_to_all | solution.py:42
  488.4 7.2 %slice_bitcast_fusion = (bf16[8,1,34,4096]{3,2,0,1:T(8,128)(2,1)}, bf16[8,1,34,4096]{3,2,0,1:T(8,128)(2,1)}, bf16[8,1,34,4096]{3,2,0,1:T(8,128)(2,1)}, bf16[8,1,34,4096]{3,2,0,1:T(8,128)(2,1)S(1)}) fusion(bf16[8,4,34,4096]{3,2,1,0:T(8,128)(2,1)} %bitcast.3), kind=kLoop, calls=%fused_computation.6 | loop fusion | bytes 17825792
  495.6 3.1 reshape_squeeze.15
  498.7 3.1 reshape_squeeze.14
  501.8 3.1 reshape_squeeze.13
  504.8 1.8 reshape_squeeze.12
  506.6 0.0 copy-start.1
  506.6 2.5 fusion.6
  509.1 0.0 copy-done.1
  509.1 0.0 copy-start
  509.1 0.8 convolution_add_fusion.2
  509.9 0.9 copy-done
  510.8 0.8 convolution_add_fusion.1
  511.5 0.9 copy-done.2
  512.4 1.7 fusion.1
  (5 shorter events, 0.1 us)
Async XLA Ops:
  6.5 338.5 %reduce-scatter.4.cloned.1.call-start = ((), (), s32[]{:S(2)}) async-start(), calls=%async_computation.2 | async-start | bytes 44564480
  355.3 7.9 %copy-start.3 = (s32[1,128,2]{1,2,0:T(2,128)S(1)}, s32[1,128,2]{1,2,0:T(2,128)}, u32[]{:S(2)}) copy-start(s32[1,128,2]{1,2,0:T(2,128)} %param.3) | copy-start | bytes 3076
  355.3 133.1 %all-to-all-start = ((bf16[32,34,4096]{2,1,0:T(8,128)(2,1)}), bf16[32,34,4096]{2,1,0:T(8,128)(2,1)}, u32[]{:S(2)}, u32[]{:S(2)}) async-start(bf16[32,34,4096]{2,1,0:T(8,128)(2,1)} %reshape.32), calls=%async_computation | async-start | bytes 20971520 | tf_op jit(solution)/shard_map/all_to_all | solution.py:42
  506.6 2.5 copy-start.1
  509.1 1.6 copy-start
  510.8 1.6 copy-start.2
Sparse Core Ops, SparseCore 0:
  42.1 302.8 reduce-scatter.3
where the time goes:
time: 528 us; the launch traced here: 521 us
  waiting for transfers between devices  427 us (81%)
  matrix products  41.2 us (8%)
  local copies, waits for them, and re-layouts  31 us (6%)
  between operations  13.5 us (3%)
  starting transfers between devices  7.84 us (1%)
    unnamed x2, waiting for transfers between devices  303 us
    all_to_all x1, waiting for transfers between devices, on_device(): lax.all_to_all(outgoing, 'expert', split_axis=0, concat_axis=0, tiled=True)  124 us
    dot_general x1, matrix products, on_device(): lax.dot_general(hidden_grad, up_weight, (((1,), (1,)), ((), ())), preferr...  35.4 us
    another operation x4, local copies, waits for them, and re-layouts, on_device(): returned[:, half_index].reshape(EXPERTS * per_send, model_width)  11 us
  transfers between devices with their start and end apart: 2, of which 2 were waited for; matrix products, arithmetic and copies ran while one was open for 0% of the time, Pallas kernels for 0%

commit v1 on v0

v1 whole, which is shorter than its diff:
```python
import functools

import jax
import jax.numpy as jnp
from jax import lax
from jax.experimental import pallas as pl
from jax.experimental.pallas import tpu as pltpu
from jax.sharding import PartitionSpec as P

EXPERTS = 8
SLOTS = 34
SHARDS = 8
BLOCK = SLOTS * SHARDS
GROUP = 4 * BLOCK
TOKENS = 128
WIDE = 256
HALF = 128
MESH = pl.DeviceIdType.MESH
BF = jnp.bfloat16
F32 = jnp.float32


def nt_dot(a, b):
    return lax.dot_general(a, b, (((1,), (1,)), ((), ())), preferred_element_type=F32)


def kernel(
    chunks, ids_ref, hid_ref, w_ref, out_ref,
    a_buf, w_buf, xs, xr, zb, ys, yr, sel, fin, keys,
    in_sem, core_send, core_recv, key_send, key_recv,
    x_send, x_recv, z_send, z_recv, y_send, y_recv, o_send, o_recv,
):
    x = lax.axis_index("dp")
    col = lax.axis_index("expert")
    z, y, k = col // 8, (col // 2) % 4, col % 2
    half_cols = chunks * WIDE
    hid = hid_ref.shape[1]

    def dev(dx=0, dz=0, dy=0, dk=0):
        return ((x + dx) % 4, ((z + dz) % 4) * 8 + ((y + dy) % 4) * 2 + (k + dk) % 2)

    def rows_of(start, size):
        return pl.ds(pl.multiple_of(start, 16), size)

    def remote(src, dst, send, recv, to):
        return pltpu.make_async_remote_copy(
            src_ref=src, dst_ref=dst, send_sem=send, recv_sem=recv, device_id=to, device_id_type=MESH
        )

    group_order = [(x + 2) % 4, (x + 3) % 4, (x + 1) % 4, x]

    def local_a(i):
        rows = rows_of(group_order[i] * GROUP, GROUP)
        return pltpu.make_async_copy(hid_ref.at[rows], a_buf.at[0, rows], in_sem.at[i])

    def local_w(j):
        return pltpu.make_async_copy(
            w_ref.at[rows_of(k * half_cols + j * WIDE, WIDE)], w_buf.at[0, rows_of(j * WIDE, WIDE)], in_sem.at[4 + j]
        )

    def core_a(i):
        rows = rows_of(group_order[i] * GROUP, GROUP)
        return remote(hid_ref.at[rows], a_buf.at[1, rows], core_send.at[i], core_recv.at[i], dev(dk=1))

    def core_w(j):
        return remote(
            w_ref.at[rows_of((1 - k) * half_cols + j * WIDE, WIDE)],
            w_buf.at[1, rows_of(j * WIDE, WIDE)],
            core_send.at[4 + j], core_recv.at[4 + j], dev(dk=1),
        )

    peers = [(dy, dk) for dy in range(4) for dk in range(2) if (dy, dk) != (0, 0)]

    def key_copy(i):
        dy, dk = peers[i]
        mine = y * 2 + k
        return remote(keys.at[mine], keys.at[mine], key_send.at[i], key_recv.at[i], dev(dy=dy, dk=dk))

    def tree_copy(sends, recvs, s_sem, r_sem, axis, c, kind, side):
        step = 1 if (side == 0) != (kind == 1) else -1
        src = recvs.at[c, 0, side] if kind == 2 else sends.at[c, kind, side]
        return remote(
            src, recvs.at[c, kind, side], s_sem.at[c, kind, side], r_sem.at[c, kind, side], dev(**{axis: step})
        )

    x_copy = functools.partial(tree_copy, xs, xr, x_send, x_recv, "dx")
    y_copy = functools.partial(tree_copy, ys, yr, y_send, y_recv, "dy")

    def z_copy(c, i):
        there = (z + i + 1) % 4
        return remote(
            xr.at[c, 1, :, rows_of(there * BLOCK, BLOCK), :],
            zb.at[c, :, rows_of(z * BLOCK, BLOCK), :],
            z_send.at[c, i], z_recv.at[c, i], dev(dz=i + 1),
        )

    def o_copy(c):
        return remote(
            fin.at[c, rows_of((1 - k) * TOKENS, TOKENS)],
            out_ref.at[:, pl.ds(pl.multiple_of(k * half_cols + c * WIDE, WIDE), WIDE)],
            o_send.at[c], o_recv.at[c], dev(dk=1),
        )

    local_w(0).start()
    for i in range(4):
        local_a(i).start()
    for j in range(1, chunks):
        local_w(j).start()

    barrier = pltpu.get_barrier_semaphore()
    near = [dev(dx=1), dev(dx=3)] + [dev(dz=i) for i in (1, 2, 3)] + [dev(dy=a, dk=b) for a, b in peers]
    for to in near:
        pl.semaphore_signal(barrier, inc=1, device_id=to, device_id_type=MESH)
    pl.semaphore_wait(barrier, len(near))

    core_w(0).start()
    core_a(0).start()
    core_w(1).start()
    for i in range(1, 4):
        core_a(i).start()
    for j in range(2, chunks):
        core_w(j).start()

    ids = ids_ref[...]
    experts = lax.broadcasted_iota(jnp.int32, (EXPERTS, TOKENS), 0)
    ones = [ids[i:i + 1, :] == experts for i in range(2)]
    counts = (ones[0].astype(F32) + ones[1].astype(F32)).astype(BF)
    earlier = lax.broadcasted_iota(jnp.int32, (TOKENS, TOKENS), 0) < lax.broadcasted_iota(jnp.int32, (TOKENS, TOKENS), 1)
    before = jnp.dot(counts, earlier.astype(F32).astype(BF), preferred_element_type=F32)
    code_rows = []
    for i in range(2):
        position = jnp.sum(jnp.where(ones[i], before, 0.0), axis=0, keepdims=True).astype(jnp.int32)
        if i == 1:
            position = position + (ids[0:1, :] == ids[1:2, :]).astype(jnp.int32)
        expert = ids[i:i + 1, :]
        code_rows.append((expert % 2) * GROUP + (expert // 2) * BLOCK + position)
    row = lax.broadcasted_iota(jnp.int32, (8, TOKENS), 0)
    keys[y * 2 + k] = jnp.where(row == 0, code_rows[0], code_rows[1])
    for i in range(7):
        key_copy(i).start()

    def product(g, c, r):
        rows = rows_of(g * GROUP + r * BLOCK, BLOCK)
        cols = rows_of(c * WIDE, WIDE)
        return nt_dot(a_buf[0, rows, :], w_buf[0, cols, :]) + nt_dot(a_buf[1, rows, :], w_buf[1, cols, :])

    def tiles(body):
        lax.fori_loop(0, 4, lambda r, _: (body(r), 0)[1], 0)

    def wait_a(i):
        local_a(i).wait()
        core_a(i).wait_recv()

    def s0(c):
        local_w(c).wait()
        core_w(c).wait_recv()

        @pl.when(c == 0)
        def _():
            wait_a(0)

        def body(r):
            acc = product((x + 2) % 4, c, r)
            rows = rows_of(r * BLOCK, BLOCK)
            xs[c, 0, 0, rows, :] = acc[:, :HALF].astype(BF)
            xs[c, 0, 1, rows, :] = acc[:, HALF:].astype(BF)

        tiles(body)
        x_copy(c, 0, 0).start()
        x_copy(c, 0, 1).start()

    def s1(c):
        for i, side in ((1, 0), (2, 1)):
            @pl.when(c == 0)
            def _():
                wait_a(i)

            other = 1 - side
            g = (x + 3) % 4 if side == 0 else (x + 1) % 4
            x_copy(c, 0, other).wait_recv()

            def body(r):
                acc = product(g, c, r)
                rows = rows_of(r * BLOCK, BLOCK)
                part = [acc[:, :HALF], acc[:, HALF:]]
                xs[c, 1, side, rows, :] = part[side].astype(BF)
                xr[c, 0, other, rows, :] = (part[other] + xr[c, 0, other, rows, :].astype(F32)).astype(BF)

            tiles(body)
            x_copy(c, 2, other).start()
            x_copy(c, 1, side).start()

    def s2(c):
        @pl.when(c == 0)
        def _():
            wait_a(3)

        for side in range(2):
            x_copy(c, 1, side).wait_recv()
            x_copy(c, 2, side).wait_recv()

        def body(r):
            acc = product(x, c, r)
            rows = rows_of(r * BLOCK, BLOCK)
            for side in range(2):
                part = acc[:, side * HALF:(side + 1) * HALF]
                total = part + (xr[c, 1, side, rows, :].astype(F32) + xr[c, 2, side, rows, :].astype(F32))
                xr[c, 1, side, rows, :] = total.astype(BF)

        tiles(body)
        for i in range(3):
            z_copy(c, i).start()
        mine = rows_of(z * BLOCK, BLOCK)
        zb[c, :, mine, :] = xr[c, 1, :, mine, :]

    def tokens_of(c, yy):
        chosen = sel[rows_of(yy * 2 * TOKENS, 2 * TOKENS), :]
        values = jnp.concatenate([zb[c, 0], zb[c, 1]], axis=1)
        return jnp.dot(chosen, values, preferred_element_type=F32)

    def s3(c):
        @pl.when(c == 0)
        def _():
            for i in range(7):
                key_copy(i).wait_recv()
            lanes = lax.broadcasted_iota(jnp.int32, (TOKENS, GROUP), 1).astype(F32)

            def build(s, _):
                turned = jnp.transpose(keys[s].astype(F32))
                shift = (s * SLOTS - (y // 2) * GROUP).astype(F32)
                hit = (turned[:, 0:1] + shift == lanes) | (turned[:, 1:2] + shift == lanes)
                sel[rows_of(s * TOKENS, TOKENS), :] = hit.astype(F32).astype(BF)
                return 0

            lax.fori_loop(0, SHARDS, build, 0)

        for i in range(3):
            z_copy(c, i).wait_recv()
        acc = tokens_of(c, (y + 2) % 4)
        ys[c, 0, 0] = acc[:, :HALF].astype(BF)
        ys[c, 0, 1] = acc[:, HALF:].astype(BF)
        y_copy(c, 0, 0).start()
        y_copy(c, 0, 1).start()

    def s4(c):
        for side in range(2):
            other = 1 - side
            acc = tokens_of(c, (y + 3) % 4 if side == 0 else (y + 1) % 4)
            part = [acc[:, :HALF], acc[:, HALF:]]
            ys[c, 1, side] = part[side].astype(BF)
            y_copy(c, 1, side).start()
            y_copy(c, 0, other).wait_recv()
            yr[c, 0, other] = (part[other] + yr[c, 0, other].astype(F32)).astype(BF)
            y_copy(c, 2, other).start()

    def s5(c):
        acc = tokens_of(c, y)
        for side in range(2):
            y_copy(c, 1, side).wait_recv()
            y_copy(c, 2, side).wait_recv()
            part = acc[:, side * HALF:(side + 1) * HALF]
            total = part + (yr[c, 1, side].astype(F32) + yr[c, 2, side].astype(F32))
            fin[c, :, side * HALF:(side + 1) * HALF] = total.astype(BF)
        o_copy(c).start()
        cols = pl.ds(pl.multiple_of(k * half_cols + c * WIDE, WIDE), WIDE)
        out_ref[:, cols] = fin[c, rows_of(k * TOKENS, TOKENS), :]

    def step(i, _):
        for lag, stage in ((0, s0), (1, s1), (3, s3), (4, s4), (5, s5), (2, s2)):
            @pl.when((i >= lag) & (i - lag < chunks))
            def _():
                stage(i - lag)
        return 0

    lax.fori_loop(0, chunks + 5, step, 0)

    def finish(c, _):
        core_w(c).wait_send()
        for kind in range(3):
            for side in range(2):
                x_copy(c, kind, side).wait_send()
                y_copy(c, kind, side).wait_send()
        for i in range(3):
            z_copy(c, i).wait_send()
        o_copy(c).wait()
        return 0

    lax.fori_loop(0, chunks, finish, 0)
    for i in range(4):
        core_a(i).wait_send()
    for i in range(7):
        key_copy(i).wait_send()


def on_device(expert_ids, hidden_grad, up_weight):
    rows, hid = hidden_grad.shape
    width = up_weight.shape[0]
    chunks = width // 2 // WIDE
    dma = pltpu.SemaphoreType.DMA
    out = pl.pallas_call(
        functools.partial(kernel, chunks),
        out_shape=jax.ShapeDtypeStruct((TOKENS, width), BF),
        in_specs=[
            pl.BlockSpec(memory_space=pltpu.VMEM),
            pl.BlockSpec(memory_space=pl.ANY),
            pl.BlockSpec(memory_space=pl.ANY),
        ],
        out_specs=pl.BlockSpec(memory_space=pltpu.VMEM),
        scratch_shapes=[
            pltpu.VMEM((2, rows, hid), BF),
            pltpu.VMEM((2, width // 2, hid), BF),
            pltpu.VMEM((chunks, 2, 2, GROUP, HALF), BF),
            pltpu.VMEM((chunks, 3, 2, GROUP, HALF), BF),
            pltpu.VMEM((chunks, 2, GROUP, HALF), BF),
            pltpu.VMEM((chunks, 2, 2, 2 * TOKENS, HALF), BF),
            pltpu.VMEM((chunks, 3, 2, 2 * TOKENS, HALF), BF),
            pltpu.VMEM((SHARDS * TOKENS, GROUP), BF),
            pltpu.VMEM((chunks, 2 * TOKENS, WIDE), BF),
            pltpu.VMEM((SHARDS, 8, TOKENS), jnp.int32),
            dma((4 + chunks,)), dma((4 + chunks,)), dma((4 + chunks,)),
            dma((7,)), dma((7,)),
            dma((chunks, 3, 2)), dma((chunks, 3, 2)),
            dma((chunks, 3)), dma((chunks, 3)),
            dma((chunks, 3, 2)), dma((chunks, 3, 2)),
            dma((chunks,)), dma((chunks,)),
        ],
        compiler_params=pltpu.CompilerParams(
            collective_id=0, has_side_effects=True, vmem_limit_bytes=63 * 2**20
        ),
        cost_estimate=pl.CostEstimate(
            flops=2 * rows * hid * width, bytes_accessed=2 * (rows + width) * hid + 2 * TOKENS * width, transcendentals=0
        ),
        name="up_cotangent",
    )(expert_ids[0].T, hidden_grad, up_weight)
    return out[None]


def solution(mesh):
    return jax.shard_map(
        on_device,
        mesh=mesh,
        in_specs=(P("dp", "expert", None), P(None, ("dp", "expert")), P(None, ("dp", "expert"))),
        out_specs=P("dp", "expert", None),
        check_vma=False,
    )
```

time: 528 us -> 188 us (0.36); the launches traced: 521 us -> 187 us
  waiting for transfers between devices: 427 us -> 0 us
  Pallas kernels: 0 us -> 185 us
  matrix products: 41.2 us -> 0 us
  local copies, waits for them, and re-layouts: 31 us -> 2.29 us
  between operations: 13.5 us -> 0.01 us
  starting transfers between devices: 7.84 us -> 0 us
    unnamed x2 -> x0, waiting for transfers between devices: 303 us -> none
    pallas_call x0 -> x1, Pallas kernels: none -> 185 us  [on_device(): pl.pallas_call(functools.partial(kernel, chunks), out_shape=jax.ShapeDtyp...]
    all_to_all x1 -> x0, waiting for transfers between devices: 124 us -> none  [on_device(): lax.all_to_all(outgoing, 'expert', split_axis=0, concat_axis=0, tiled=True)]
    dot_general x5 -> x0, matrix products: 41.2 us -> none  [the longest x1 35.4 us: on_device(): lax.dot_general(hidden_grad, up_weight, (((1,), (1,)), ((), ())), preferr...]
    another operation x5 -> x0, local copies, waits for them, and re-layouts: 11 us -> none  [the longest x4 11 us: on_device(): returned[:, half_index].reshape(EXPERTS * per_send, model_width)]
    reshape x3 -> x0, local copies, waits for them, and re-layouts: 10.5 us -> none  [the longest x1 10.3 us: on_device(): outgoing = summed.reshape(columns, per_send, model_width)]
    all_to_all x1 -> x0, starting transfers between devices: 7.84 us -> none  [on_device(): lax.all_to_all(outgoing, 'expert', split_axis=0, concat_axis=0, tiled=True)]
    unnamed x10 -> x1, local copies, waits for them, and re-layouts: 9.06 us -> 2.29 us
  transfers between devices with their start and end apart: 2 -> 0, of which waited for: 2 -> 0; matrix products, arithmetic and copies ran while one was open for 0% -> 0% of each run, Pallas kernels for 0% -> 0%
where the time goes in v1:
time: 188 us; the launch traced here: 187 us
  Pallas kernels  185 us (98%)
  local copies, waits for them, and re-layouts  2.29 us (1%)
    pallas_call x1, Pallas kernels, on_device(): pl.pallas_call(functools.partial(kernel, chunks), out_shape=jax.ShapeDtyp...  185 us

profile of v1, /device:TPU:1, one launch (start us, length us, event | category | flops | bytes accessed | tf_op | source)
XLA Modules:
  0.0 187.5 jit_solution(12668746801176305839)
XLA Ops:
  0.0 185.2 %up_cotangent.1 = bf16[128,4096]{1,0:T(8,128)(2,1)} custom-call(s32[2,128]{1,0:T(2,128)} %bitcast.5, bf16[4352,768]{1,0:T(8,128)(2,1)} %hid_ref.1, bf16[4096,768]{1,0:T(8,128)(2,1)} %w_ref.1), custom_call_target="tpu_custom_call" | custom-call | flops 27380416512 | bytes 14024704 | tf_op jit(solution)/shard_map/up_cotangent/pallas_call | solution.py:300
  185.2 2.3 %copy.5 = bf16[1,128,4096]{2,1,0:T(8,128)(2,1)} copy(bf16[1,128,4096]{2,1,0:T(8,128)(2,1)} %bitcast.4) | data formatting | bytes 2097152

commit v2 on v1

v2 whole, which is shorter than its diff:
```python
import functools

import jax
import jax.numpy as jnp
from jax import lax
from jax.experimental import pallas as pl
from jax.experimental.pallas import tpu as pltpu
from jax.sharding import PartitionSpec as P

EXPERTS = 8
SLOTS = 34
SHARDS = 8
BLOCK = SLOTS * SHARDS
GROUP = 4 * BLOCK
WINDOW = 80
DEPTH = 4 * WINDOW
TOKENS = 128
WIDE = 256
HALF = 128
MESH = pl.DeviceIdType.MESH
BF = jnp.bfloat16
F32 = jnp.float32


def nt_dot(a, b):
    return lax.dot_general(a, b, (((1,), (1,)), ((), ())), preferred_element_type=F32)


def kernel(
    direct, early, ids_ref, hid_ref, w_ref, out_ref,
    a_buf, w_buf, xs, xr, zb, ys, yr, zs2, zb2, ys2, yr2, ye2, xr2, sel, fin, keys,
    in_sem, core_send, core_recv, key_sem, xt_send, xp_send, xc_send, xt_recv, x_recv,
    z_send, z_recv, y_send, yt_recv, y_recv, z2_send, z2_recv, y2_send, y2t_recv, y2_recv, x2_send, x2t_recv, x2_recv, o_sem,
):
    x = lax.axis_index("dp")
    col = lax.axis_index("expert")
    z, y, k = col // 8, (col // 2) % 4, col % 2
    chunks = direct + early
    half_cols = chunks * WIDE
    slots_x = xs.shape[0]
    slots_z = zs2.shape[0]

    def dev(dx=0, dz=0, dy=0, dk=0):
        return ((x + dx) % 4, ((z + dz) % 4) * 8 + ((y + dy) % 4) * 2 + (k + dk) % 2)

    def rows_of(start, size):
        return pl.ds(pl.multiple_of(start, 16), size)

    def remote(src, dst, send, recv, to):
        return pltpu.make_async_remote_copy(
            src_ref=src, dst_ref=dst, send_sem=send, recv_sem=recv, device_id=to, device_id_type=MESH
        )

    def loop(count, body):
        lax.fori_loop(0, count, lambda i, _: (body(i), 0)[1], 0)

    def nth_group(i):
        return (x + jnp.where(i < 2, i + 2, 3 - i)) % 4

    def local_a(i):
        rows = rows_of(nth_group(i) * GROUP, GROUP)
        return pltpu.make_async_copy(hid_ref.at[rows], a_buf.at[0, rows], in_sem.at[i])

    def local_w(j):
        return pltpu.make_async_copy(
            w_ref.at[rows_of(k * half_cols + j * WIDE, WIDE)], w_buf.at[0, rows_of(j * WIDE, WIDE)], in_sem.at[4 + j]
        )

    def core_a(i):
        rows = rows_of(nth_group(i) * GROUP, GROUP)
        return remote(hid_ref.at[rows], a_buf.at[1, rows], core_send.at[0], core_recv.at[i], dev(dk=1))

    def core_w(j):
        return remote(
            w_ref.at[rows_of((1 - k) * half_cols + j * WIDE, WIDE)],
            w_buf.at[1, rows_of(j * WIDE, WIDE)],
            core_send.at[1], core_recv.at[4 + j], dev(dk=1),
        )

    peers = [(dy, dk) for dy in range(4) for dk in range(2) if (dy, dk) != (0, 0)]

    def key_copy(i):
        dy, dk = peers[i]
        mine = y * 2 + k
        return remote(keys.at[x, mine], keys.at[x, mine], key_sem.at[0], key_sem.at[1], dev(dy=dy, dk=dk))

    def group_copy(i):
        return remote(keys.at[x], keys.at[x], key_sem.at[2], key_sem.at[3], dev(dx=i + 1))

    def wait_bytes(ref, sem):
        pltpu.make_async_copy(ref, ref, sem).wait()

    def tree_copy(source, recvs, s_sems, t_sem, r_sem, axis, c, kind, side):
        step = 1 if (side == 0) != (kind == 1) else -1
        src = recvs.at[c, 0, side] if kind == 2 else source(c, kind, side, step)
        return remote(
            src, recvs.at[c, kind, side], s_sems[kind].at[c],
            t_sem.at[c, side] if kind == 0 else r_sem.at[c], dev(**{axis: step}),
        )

    x_copy = functools.partial(
        tree_copy, lambda c, kind, side, step: xs.at[c % slots_x, kind, side], xr,
        (xt_send, xp_send, xc_send), xt_recv, x_recv, "dx",
    )
    y_copy = functools.partial(
        tree_copy, lambda c, kind, side, step: ys.at[c, kind, side], yr, (y_send,) * 3, yt_recv, y_recv, "dy"
    )
    y2_copy = functools.partial(
        tree_copy, lambda c, kind, side, step: ys2.at[c, kind, side], yr2, (y2_send,) * 3, y2t_recv, y2_recv, "dy"
    )
    x2_copy = functools.partial(
        tree_copy, lambda c, kind, side, step: ye2.at[c, (x + (step if kind else 2)) % 4, side], xr2,
        (x2_send,) * 3, x2t_recv, x2_recv, "dx",
    )

    def wait_through(recvs, t_sem, c, side):
        wait_bytes(recvs.at[c, 0, side], t_sem.at[c, side])

    def wait_tree(recvs, r_sem, c):
        wait_bytes(recvs.at[c, pl.ds(1, 2)], r_sem.at[c])

    def z_copy(c, i):
        there = (z + i + 1) % 4
        return remote(
            xr.at[c, 1, :, rows_of(there * BLOCK, BLOCK), :], zb.at[c, z], z_send.at[c], z_recv.at[c], dev(dz=i + 1)
        )

    def z2_copy(c, g, dz):
        there = rows_of(((z + dz) % 4) * BLOCK, BLOCK)
        return remote(
            zs2.at[c % slots_z, g, :, there, :], zb2.at[c, z, g], z2_send.at[c, g], z2_recv.at[c], dev(dz=dz)
        )

    def wait_z2_sent(c, g):
        wait_bytes(zs2.at[c % slots_z, g, :, pl.ds(0, 3 * BLOCK), :], z2_send.at[c, g])

    def out_cols(c):
        return out_ref.at[:, pl.ds(pl.multiple_of(k * half_cols + c * WIDE, WIDE), WIDE)]

    def o_copy(c):
        return remote(fin.at[c, rows_of((1 - k) * TOKENS, TOKENS)], out_cols(c), o_sem.at[0], o_sem.at[1], dev(dk=1))

    def o_local(c):
        return pltpu.make_async_copy(fin.at[c, rows_of(k * TOKENS, TOKENS)], out_cols(c), o_sem.at[2])

    for j in (direct, 0, 1):
        local_w(j).start()
    for i in range(4):
        local_a(i).start()
    rest = [j for j in range(2, chunks) if j != direct]
    for j in rest:
        local_w(j).start()

    barrier = pltpu.get_barrier_semaphore()
    near = [dev(dx=i) for i in (1, 2, 3)] + [dev(dz=i) for i in (1, 2, 3)] + [dev(dy=a, dk=b) for a, b in peers]
    for to in near:
        pl.semaphore_signal(barrier, inc=1, device_id=to, device_id_type=MESH)

    ids = ids_ref[...]
    experts = lax.broadcasted_iota(jnp.int32, (EXPERTS, TOKENS), 0)
    ones = [ids[i:i + 1, :] == experts for i in range(2)]
    counts = (ones[0].astype(F32) + ones[1].astype(F32)).astype(BF)
    earlier = lax.broadcasted_iota(jnp.int32, (TOKENS, TOKENS), 0) < lax.broadcasted_iota(jnp.int32, (TOKENS, TOKENS), 1)
    before = jnp.dot(counts, earlier.astype(F32).astype(BF), preferred_element_type=F32)
    code_rows = []
    for i in range(2):
        position = jnp.sum(jnp.where(ones[i], before, 0.0), axis=0, keepdims=True).astype(jnp.int32)
        if i == 1:
            position = position + (ids[0:1, :] == ids[1:2, :]).astype(jnp.int32)
        expert = ids[i:i + 1, :]
        code_rows.append((expert % 2) * DEPTH + (expert // 2) * WINDOW + position)
    row = lax.broadcasted_iota(jnp.int32, (8, TOKENS), 0)
    keys[x, y * 2 + k] = jnp.where(row == 0, code_rows[0], code_rows[1])

    pl.semaphore_wait(barrier, len(near))
    core_w(direct).start()
    core_a(0).start()
    for j in (0, 1):
        core_w(j).start()
    for i in range(7):
        key_copy(i).start()
    for i in range(1, 4):
        core_a(i).start()
    for j in rest:
        core_w(j).start()

    def product(g, c):
        rows = rows_of(g * GROUP, GROUP)
        cols = rows_of(c * WIDE, WIDE)
        return nt_dot(a_buf[0, rows, :], w_buf[0, cols, :]) + nt_dot(a_buf[1, rows, :], w_buf[1, cols, :])

    def wait_a(i):
        local_a(i).wait()
        core_a(i).wait_recv()

    def wait_w(c):
        local_w(c).wait()
        core_w(c).wait_recv()

    def halves(acc):
        return [acc[:, :HALF], acc[:, HALF:]]

    def a0(c):
        wait_w(c)

        @pl.when(c >= slots_x)
        def _():
            wait_bytes(xs.at[c % slots_x, 0], xt_send.at[c - slots_x])

        for side, part in enumerate(halves(product((x + 2) % 4, c))):
            xs[c % slots_x, 0, side] = part.astype(BF)
            x_copy(c, 0, side).start()

    def a1(side, c):
        other = 1 - side

        if side == 0:
            @pl.when(c >= slots_x)
            def _():
                wait_bytes(xs.at[c % slots_x, 1], xp_send.at[c - slots_x])

        wait_through(xr, xt_recv, c, other)
        part = halves(product((x + 3) % 4 if side == 0 else (x + 1) % 4, c))
        xr[c, 0, other] = (part[other] + xr[c, 0, other].astype(F32)).astype(BF)
        xs[c % slots_x, 1, side] = part[side].astype(BF)
        x_copy(c, 2, other).start()
        x_copy(c, 1, side).start()

    def a2(c):
        wait_tree(xr, x_recv, c)
        for side, part in enumerate(halves(product(x, c))):
            total = part + (xr[c, 1, side].astype(F32) + xr[c, 2, side].astype(F32))
            xr[c, 1, side] = total.astype(BF)
        for i in range(3):
            z_copy(c, i).start()
        zb[c, z] = xr[c, 1, :, rows_of(z * BLOCK, BLOCK), :]

    def to_tokens(blocks, g, yy):
        rows = rows_of(yy * 64, WINDOW)
        values = jnp.concatenate(
            [jnp.concatenate([blocks(e)[side, rows, :] for e in range(4)], axis=0) for side in range(2)], axis=1
        )
        return jnp.dot(sel[g, yy], values, preferred_element_type=F32)

    def a_tokens(c, yy):
        return to_tokens(lambda e: zb.at[c, e], x, yy)

    def share_keys(_):
        wait_bytes(keys.at[x, pl.ds(0, 7)], key_sem.at[1])
        for i in range(3):
            group_copy(i).start()

    def build(part):
        @pl.when(part == 0)
        def _():
            wait_bytes(keys.at[pl.ds(0, 3)], key_sem.at[3])

        lanes = lax.broadcasted_iota(jnp.int32, (TOKENS, DEPTH), 1).astype(F32)

        def body(n):
            g, yy, kk = part, n // 2, n % 2
            turned = jnp.transpose(keys[g, yy * 2 + kk].astype(F32))
            shift = (yy * 4 + kk * SLOTS - (y // 2) * DEPTH).astype(F32)
            hit = (turned[:, 0:1] + shift == lanes) | (turned[:, 1:2] + shift == lanes)
            sel[g, yy, rows_of(kk * TOKENS, TOKENS), :] = hit.astype(F32).astype(BF)

        loop(8, body)

    def a3(c):
        wait_bytes(zb.at[c, pl.ds(0, 3)], z_recv.at[c])
        for side, part in enumerate(halves(a_tokens(c, (y + 2) % 4))):
            ys[c, 0, side] = part.astype(BF)
        y_copy(c, 0, 0).start()
        y_copy(c, 0, 1).start()

    def a4(c):
        for side in range(2):
            other = 1 - side
            part = halves(a_tokens(c, (y + 3) % 4 if side == 0 else (y + 1) % 4))
            ys[c, 1, side] = part[side].astype(BF)
            y_copy(c, 1, side).start()
            wait_through(yr, yt_recv, c, other)
            yr[c, 0, other] = (part[other] + yr[c, 0, other].astype(F32)).astype(BF)
            y_copy(c, 2, other).start()

    def deliver(c):
        o_copy(c).start()
        o_local(c).start()

    def a5(c):
        wait_tree(yr, y_recv, c)
        for side, part in enumerate(halves(a_tokens(c, y))):
            total = part + (yr[c, 1, side].astype(F32) + yr[c, 2, side].astype(F32))
            fin[c, :, side * HALF:(side + 1) * HALF] = total.astype(BF)
        deliver(c)

    def a6(c):
        wait_bytes(xr.at[c, 0], xc_send.at[c])
        wait_bytes(yr.at[c], y_send.at[c])
        wait_bytes(xr.at[c, 1, :, pl.ds(0, 3 * BLOCK), :], z_send.at[c])

    def e0(q):
        c, i = q // 4, q % 4
        g = nth_group(i)

        @pl.when(i == 0)
        def _():
            wait_w(direct + c)

        @pl.when(c == 0)
        def _():
            wait_a(i)

        @pl.when(c >= slots_z)
        def _():
            wait_z2_sent(c - slots_z, g)

        for side, part in enumerate(halves(product(g, direct + c))):
            zs2[c % slots_z, g, side] = part.astype(BF)
        for dz in (2, 1, 3):
            z2_copy(c, g, dz).start()
        zb2[c, z, g] = zs2[c % slots_z, g, :, rows_of(z * BLOCK, BLOCK), :]

    def e_tokens(c, g, yy):
        return to_tokens(lambda e: zb2.at[c, e, g], g, yy)

    def group_rows(g):
        return rows_of(g * 2 * TOKENS, 2 * TOKENS)

    def e1(c):
        wait_bytes(zb2.at[c, pl.ds(0, 3)], z2_recv.at[c])

        def body(g):
            for side, part in enumerate(halves(e_tokens(c, g, (y + 2) % 4))):
                ys2[c, 0, side, group_rows(g), :] = part.astype(BF)

        loop(4, body)
        y2_copy(c, 0, 0).start()
        y2_copy(c, 0, 1).start()

    def e2(c):
        for side in range(2):
            other = 1 - side
            wait_through(yr2, y2t_recv, c, other)

            def body(g):
                part = halves(e_tokens(c, g, (y + 3) % 4 if side == 0 else (y + 1) % 4))
                rows = group_rows(g)
                ys2[c, 1, side, rows, :] = part[side].astype(BF)
                yr2[c, 0, other, rows, :] = (part[other] + yr2[c, 0, other, rows, :].astype(F32)).astype(BF)

            loop(4, body)
            y2_copy(c, 2, other).start()
            y2_copy(c, 1, side).start()

    def e3(c):
        wait_tree(yr2, y2_recv, c)

        def body(g):
            rows = group_rows(g)
            for side, part in enumerate(halves(e_tokens(c, g, y))):
                total = part + (yr2[c, 1, side, rows, :].astype(F32) + yr2[c, 2, side, rows, :].astype(F32))
                ye2[c, g, side] = total.astype(BF)

        loop(4, body)
        for kind in range(2):
            for side in range(2):
                x2_copy(c, kind, side).start()

    def e4(c):
        for side in range(2):
            wait_through(xr2, x2t_recv, c, side)
            mine = ye2[c, (x + 1) % 4 if side == 0 else (x + 3) % 4, side]
            xr2[c, 0, side] = (mine.astype(F32) + xr2[c, 0, side].astype(F32)).astype(BF)
            x2_copy(c, 2, side).start()

    def e5(c):
        wait_tree(xr2, x2_recv, c)
        for side in range(2):
            total = ye2[c, x, side].astype(F32) + (xr2[c, 1, side].astype(F32) + xr2[c, 2, side].astype(F32))
            fin[direct + c, :, side * HALF:(side + 1) * HALF] = total.astype(BF)
        deliver(direct + c)

    def e6(c):
        wait_bytes(xr2.at[c], x2_send.at[c])
        wait_bytes(yr2.at[c], y2_send.at[c])

    def old_sends(_):
        wait_bytes(a_buf.at[1], core_send.at[0])
        wait_bytes(w_buf.at[1], core_send.at[1])
        wait_bytes(keys.at[x, pl.ds(0, 7)], key_sem.at[0])
        wait_bytes(keys.at[pl.ds(0, 3)], key_sem.at[2])

    def last_sends(_):
        for c in range(max(0, direct - slots_x), direct):
            wait_bytes(xs.at[c % slots_x, 0], xt_send.at[c])
            wait_bytes(xs.at[c % slots_x, 1], xp_send.at[c])
        for c in range(max(0, early - slots_z), early):
            for g in range(4):
                wait_z2_sent(c, g)

    plan = (
        (a0, (2, 3, 6, 10, 17)),
        (functools.partial(a1, 0), (11, 19, 20, 24, 25)),
        (functools.partial(a1, 1), (11, 19, 20, 24, 25)),
        (e0, (0, 3, 5, 7, 8, 9, 15, 16, 17, 21, 22, 27)),
        (share_keys, (1,)),
        (build, (4, 9, 12, 13)),
        (e1, (14, 23, 30)),
        (e2, (18, 26, 33)),
        (e3, (29, 39, 44)),
        (e4, (38, 42, 48)),
        (e5, (41, 49, 53)),
        (a2, (28, 31, 34, 35, 37)),
        (a3, (32, 34, 36, 43, 47)),
        (a4, (35, 40, 45, 50, 52)),
        (a5, (46, 51, 54, 55, 56)),
        (old_sends, (32,)),
        (last_sends, (41,)),
        (e6, (43, 51, 55)),
        (a6, (48, 53, 55, 56, 57)),
    )

    def step(n):
        for stage, steps in plan:
            now = [n == at for at in steps]

            @pl.when(functools.reduce(jnp.logical_or, now))
            def _():
                stage(sum(i * hit.astype(jnp.int32) for i, hit in enumerate(now)))

    loop(1 + max(max(steps) for _, steps in plan), step)
    mine = fin.at[:, pl.ds(0, TOKENS)]
    for i in range(3):
        wait_bytes(mine, o_sem.at[i])


def on_device(expert_ids, hidden_grad, up_weight):
    rows, hid = hidden_grad.shape
    width = up_weight.shape[0]
    chunks = width // 2 // WIDE
    early = 3
    direct = chunks - early
    dma = pltpu.SemaphoreType.DMA
    both = 2 * TOKENS

    def vmem(*shape):
        return pltpu.VMEM(shape, BF)

    out = pl.pallas_call(
        functools.partial(kernel, direct, early),
        out_shape=jax.ShapeDtypeStruct((TOKENS, width), BF),
        in_specs=[
            pl.BlockSpec(memory_space=pltpu.VMEM),
            pl.BlockSpec(memory_space=pl.ANY),
            pl.BlockSpec(memory_space=pl.ANY),
        ],
        out_specs=pl.BlockSpec(memory_space=pl.ANY),
        scratch_shapes=[
            vmem(2, rows, hid),
            vmem(2, width // 2, hid),
            vmem(3, 2, 2, GROUP, HALF),
            vmem(direct, 3, 2, GROUP, HALF),
            vmem(direct, 4, 2, BLOCK, HALF),
            vmem(direct, 2, 2, both, HALF),
            vmem(direct, 3, 2, both, HALF),
            vmem(2, 4, 2, GROUP, HALF),
            vmem(early, 4, 4, 2, BLOCK, HALF),
            vmem(early, 2, 2, 4 * both, HALF),
            vmem(early, 3, 2, 4 * both, HALF),
            vmem(early, 4, 2, both, HALF),
            vmem(early, 3, 2, both, HALF),
            vmem(4, 4, both, DEPTH),
            vmem(chunks, both, WIDE),
            pltpu.VMEM((4, SHARDS, 8, TOKENS), jnp.int32),
            dma((4 + chunks,)), dma((2,)), dma((4 + chunks,)), dma((4,)),
            dma((direct,)), dma((direct,)), dma((direct,)), dma((direct, 2)), dma((direct,)),
            dma((direct,)), dma((direct,)), dma((direct,)), dma((direct, 2)), dma((direct,)),
            dma((early, 4)), dma((early,)), dma((early,)), dma((early, 2)), dma((early,)),
            dma((early,)), dma((early, 2)), dma((early,)), dma((3,)),
        ],
        compiler_params=pltpu.CompilerParams(
            collective_id=0, has_side_effects=True, vmem_limit_bytes=63 * 2**20
        ),
        cost_estimate=pl.CostEstimate(
            flops=2 * rows * hid * width, bytes_accessed=2 * (rows + width) * hid + 2 * TOKENS * width, transcendentals=0
        ),
        name="up_cotangent",
    )(expert_ids[0].T, hidden_grad, up_weight)
    return out[None]


def solution(mesh):
    return jax.shard_map(
        on_device,
        mesh=mesh,
        in_specs=(P("dp", "expert", None), P(None, ("dp", "expert")), P(None, ("dp", "expert"))),
        out_specs=P("dp", "expert", None),
        check_vma=False,
    )
```

time: 188 us -> 136 us (0.72)
  Pallas kernels: 185 us -> 133 us
    pallas_call x1, Pallas kernels: 185 us -> 133 us  [on_device(): pl.pallas_call(functools.partial(kernel, direct, early), out_shape=jax.Sh...]
where the time goes in v2:
time: 136 us
  Pallas kernels  133 us (98%)
  local copies, waits for them, and re-layouts  2.29 us (2%)
    pallas_call x1, Pallas kernels, on_device(): pl.pallas_call(functools.partial(kernel, direct, early), out_shape=jax.Sh...  133 us

profile of v2, /device:TPU:1, one launch (start us, length us, event | category | flops | bytes accessed | tf_op | source)
XLA Modules:
  0.0 135.6 jit_solution(12199173157436426797)
XLA Ops:
  0.0 133.3 %up_cotangent.1 = bf16[128,4096]{1,0:T(8,128)(2,1)} custom-call(s32[2,128]{1,0:T(2,128)} %bitcast.5, bf16[4352,768]{1,0:T(8,128)(2,1)} %hid_ref.1, bf16[4096,768]{1,0:T(8,128)(2,1)} %w_ref.1), custom_call_target="tpu_custom_call" | custom-call | flops 27380416512 | bytes 14024704 | tf_op jit(solution)/shard_map/up_cotangent/pallas_call | solution.py:450
  133.3 2.3 %copy.5 = bf16[1,128,4096]{2,1,0:T(8,128)(2,1)} copy(bf16[1,128,4096]{2,1,0:T(8,128)(2,1)} %bitcast.4) | data formatting | bytes 2097152

commit v3 on v2

--- a/solution.py
+++ b/solution.py
@@ -28,9 +28,9 @@
 
 def kernel(
     direct, early, ids_ref, hid_ref, w_ref, out_ref,
-    a_buf, w_buf, xs, xr, zb, ys, yr, zs2, zb2, ys2, yr2, ye2, xr2, sel, fin, keys,
+    a_buf, w_buf, xs, xr, zb, yr, zs2, zb2, ys2, yr2, ye2, xr2, sel, fin, keys,
     in_sem, core_send, core_recv, key_sem, xt_send, xp_send, xc_send, xt_recv, x_recv,
-    z_send, z_recv, y_send, yt_recv, y_recv, z2_send, z2_recv, y2_send, y2t_recv, y2_recv, x2_send, x2t_recv, x2_recv, o_sem,
+    z_send, z_recv, y_send, y_recv, z2_send, z2_recv, y2_send, y2t_recv, y2_recv, x2_send, x2t_recv, x2_recv, o_sem, a_sem,
 ):
     x = lax.axis_index("dp")
     col = lax.axis_index("expert")
@@ -90,27 +90,34 @@
     def wait_bytes(ref, sem):
         pltpu.make_async_copy(ref, ref, sem).wait()
 
-    def tree_copy(source, recvs, s_sems, t_sem, r_sem, axis, c, kind, side):
+    def tree_copy(source, recvs, s_sems, t_sem, r_sem, axis, by_side, c, kind, side):
         step = 1 if (side == 0) != (kind == 1) else -1
         src = recvs.at[c, 0, side] if kind == 2 else source(c, kind, side, step)
         return remote(
             src, recvs.at[c, kind, side], s_sems[kind].at[c],
-            t_sem.at[c, side] if kind == 0 else r_sem.at[c], dev(**{axis: step}),
+            t_sem.at[c, side] if kind == 0 else r_sem.at[c, side] if by_side else r_sem.at[c], dev(**{axis: step}),
         )
 
     x_copy = functools.partial(
         tree_copy, lambda c, kind, side, step: xs.at[c % slots_x, kind, side], xr,
-        (xt_send, xp_send, xc_send), xt_recv, x_recv, "dx",
+        (xt_send, xp_send, xc_send), xt_recv, x_recv, "dx", True,
     )
-    y_copy = functools.partial(
-        tree_copy, lambda c, kind, side, step: ys.at[c, kind, side], yr, (y_send,) * 3, yt_recv, y_recv, "dy"
-    )
+    def token_block(c, side, i, blocks=1):
+        return xr.at[c, 2, side, rows_of(i * TOKENS, blocks * TOKENS), :]
+
+    def y_copy(c, side, i):
+        dy, dk = peers[i]
+        return remote(
+            token_block(c, side, (y + dy) % 4 * 2 + (k + dk) % 2), yr.at[c, side, k * 4 + y],
+            y_send.at[c, side], y_recv.at[c, side], dev(dy=dy, dk=dk),
+        )
+
     y2_copy = functools.partial(
-        tree_copy, lambda c, kind, side, step: ys2.at[c, kind, side], yr2, (y2_send,) * 3, y2t_recv, y2_recv, "dy"
+        tree_copy, lambda c, kind, side, step: ys2.at[c, kind, side], yr2, (y2_send,) * 3, y2t_recv, y2_recv, "dy", False
     )
     x2_copy = functools.partial(
         tree_copy, lambda c, kind, side, step: ye2.at[c, (x + (step if kind else 2)) % 4, side], xr2,
-        (x2_send,) * 3, x2t_recv, x2_recv, "dx",
+        (x2_send,) * 3, x2t_recv, x2_recv, "dx", False,
     )
 
     def wait_through(recvs, t_sem, c, side):
@@ -119,23 +126,23 @@
     def wait_tree(recvs, r_sem, c):
         wait_bytes(recvs.at[c, pl.ds(1, 2)], r_sem.at[c])
 
-    def z_copy(c, i):
-        there = (z + i + 1) % 4
+    def z_copy(c, side, dz):
+        there = rows_of(((z + dz) % 4) * BLOCK, BLOCK)
         return remote(
-            xr.at[c, 1, :, rows_of(there * BLOCK, BLOCK), :], zb.at[c, z], z_send.at[c], z_recv.at[c], dev(dz=i + 1)
+            xr.at[c, 1, side, there, :], zb.at[c, z, side], z_send.at[c, side], z_recv.at[c, side], dev(dz=dz)
         )
 
     def z2_copy(c, g, dz):
         there = rows_of(((z + dz) % 4) * BLOCK, BLOCK)
         return remote(
-            zs2.at[c % slots_z, g, :, there, :], zb2.at[c, z, g], z2_send.at[c, g], z2_recv.at[c], dev(dz=dz)
+            zs2.at[c % slots_z, g, :, there, :], zb2.at[c, z, g], z2_send.at[c, g], z2_recv.at[c, g], dev(dz=dz)
         )
 
     def wait_z2_sent(c, g):
         wait_bytes(zs2.at[c % slots_z, g, :, pl.ds(0, 3 * BLOCK), :], z2_send.at[c, g])
 
     def out_cols(c):
-        return out_ref.at[:, pl.ds(pl.multiple_of(k * half_cols + c * WIDE, WIDE), WIDE)]
+        return out_ref.at[:, pl.ds(pl.multiple_of(k * half_cols + (direct + c) * WIDE, WIDE), WIDE)]
 
     def o_copy(c):
         return remote(fin.at[c, rows_of((1 - k) * TOKENS, TOKENS)], out_cols(c), o_sem.at[0], o_sem.at[1], dev(dk=1))
@@ -184,8 +191,8 @@
     for j in rest:
         core_w(j).start()
 
-    def product(g, c):
-        rows = rows_of(g * GROUP, GROUP)
+    def product(g, c, r=0, parts=1):
+        rows = rows_of(g * GROUP + r * (GROUP // parts), GROUP // parts)
         cols = rows_of(c * WIDE, WIDE)
         return nt_dot(a_buf[0, rows, :], w_buf[0, cols, :]) + nt_dot(a_buf[1, rows, :], w_buf[1, cols, :])
 
@@ -220,20 +227,27 @@
                 wait_bytes(xs.at[c % slots_x, 1], xp_send.at[c - slots_x])
 
         wait_through(xr, xt_recv, c, other)
-        part = halves(product((x + 3) % 4 if side == 0 else (x + 1) % 4, c))
-        xr[c, 0, other] = (part[other] + xr[c, 0, other].astype(F32)).astype(BF)
-        xs[c % slots_x, 1, side] = part[side].astype(BF)
-        x_copy(c, 2, other).start()
-        x_copy(c, 1, side).start()
-
-    def a2(c):
-        wait_tree(xr, x_recv, c)
-        for side, part in enumerate(halves(product(x, c))):
-            total = part + (xr[c, 1, side].astype(F32) + xr[c, 2, side].astype(F32))
-            xr[c, 1, side] = total.astype(BF)
-        for i in range(3):
-            z_copy(c, i).start()
-        zb[c, z] = xr[c, 1, :, rows_of(z * BLOCK, BLOCK), :]
+        def body(r):
+            part = halves(product((x + 3) % 4 if side == 0 else (x + 1) % 4, c, r, 2))
+            rows = rows_of(r * (GROUP // 2), GROUP // 2)
+            xr[c, 0, other, rows] = (part[other] + xr[c, 0, other, rows].astype(F32)).astype(BF)
+            xs[c % slots_x, 1, side, rows] = part[side].astype(BF)
+
+        loop(2, body)
+        for kind, at in ((1, 0), (2, 1)) if side == 0 else ((2, 0), (1, 1)):
+            x_copy(c, kind, at).start()
+
+    def a2(h):
+        c, side = h // 2, h % 2
+        wait_bytes(xr.at[c, pl.ds(1, 2), side], x_recv.at[c, side])
+        rows = rows_of(x * GROUP, GROUP)
+        cols = rows_of(c * WIDE + side * HALF, HALF)
+        own = nt_dot(a_buf[0, rows, :], w_buf[0, cols, :]) + nt_dot(a_buf[1, rows, :], w_buf[1, cols, :])
+        total = own + (xr[c, 1, side].astype(F32) + xr[c, 2, side].astype(F32))
+        xr[c, 1, side] = total.astype(BF)
+        for dz in (2, 1, 3):
+            z_copy(c, side, dz).start()
+        zb[c, z, side] = xr[c, 1, side, rows_of(z * BLOCK, BLOCK), :]
 
     def to_tokens(blocks, g, yy):
         rows = rows_of(yy * 64, WINDOW)
@@ -241,9 +255,6 @@
             [jnp.concatenate([blocks(e)[side, rows, :] for e in range(4)], axis=0) for side in range(2)], axis=1
         )
         return jnp.dot(sel[g, yy], values, preferred_element_type=F32)
-
-    def a_tokens(c, yy):
-        return to_tokens(lambda e: zb.at[c, e], x, yy)
 
     def share_keys(_):
         wait_bytes(keys.at[x, pl.ds(0, 7)], key_sem.at[1])
@@ -266,38 +277,38 @@
 
         loop(8, body)
 
-    def a3(c):
-        wait_bytes(zb.at[c, pl.ds(0, 3)], z_recv.at[c])
-        for side, part in enumerate(halves(a_tokens(c, (y + 2) % 4))):
-            ys[c, 0, side] = part.astype(BF)
-        y_copy(c, 0, 0).start()
-        y_copy(c, 0, 1).start()
-
-    def a4(c):
+    def a3(h):
+        c, side = h // 2, h % 2
+        wait_bytes(zb.at[c, pl.ds(0, 3), side], z_recv.at[c, side])
+
+        def body(yy):
+            rows = rows_of(yy * 64, WINDOW)
+            values = jnp.concatenate([zb[c, e, side, rows, :] for e in range(4)], axis=0)
+            acc = jnp.dot(sel[x, yy], values, preferred_element_type=F32).astype(BF)
+            token_block(c, side, yy * 2, 2)[...] = acc
+
+        loop(4, body)
+        for i in (3, 4, 1, 2, 5, 6, 0):
+            y_copy(c, side, i).start()
+        yr[c, side, k * 4 + y] = token_block(c, side, y * 2 + k)[...]
+
+    def a_local(c, side, core):
+        cols = pl.ds(pl.multiple_of(core * half_cols + c * WIDE + side * HALF, HALF), HALF)
+        return pltpu.make_async_copy(yr.at[c, side, core * 4], out_ref.at[:, cols], a_sem.at[0])
+
+    def a4(h):
+        c, side = h // 2, h % 2
+        wait_bytes(yr.at[c, side, pl.ds(0, 7)], y_recv.at[c, side])
+        for core in range(2):
+            parts = [yr[c, side, core * 4 + i].astype(F32) for i in range(4)]
+            yr[c, side, core * 4] = ((parts[0] + parts[1]) + (parts[2] + parts[3])).astype(BF)
+            a_local(c, side, core).start()
+
+    def a5(c):
+        wait_bytes(xr.at[c, 0], xc_send.at[c])
         for side in range(2):
-            other = 1 - side
-            part = halves(a_tokens(c, (y + 3) % 4 if side == 0 else (y + 1) % 4))
-            ys[c, 1, side] = part[side].astype(BF)
-            y_copy(c, 1, side).start()
-            wait_through(yr, yt_recv, c, other)
-            yr[c, 0, other] = (part[other] + yr[c, 0, other].astype(F32)).astype(BF)
-            y_copy(c, 2, other).start()
-
-    def deliver(c):
-        o_copy(c).start()
-        o_local(c).start()
-
-    def a5(c):
-        wait_tree(yr, y_recv, c)
-        for side, part in enumerate(halves(a_tokens(c, y))):
-            total = part + (yr[c, 1, side].astype(F32) + yr[c, 2, side].astype(F32))
-            fin[c, :, side * HALF:(side + 1) * HALF] = total.astype(BF)
-        deliver(c)
-
-    def a6(c):
-        wait_bytes(xr.at[c, 0], xc_send.at[c])
-        wait_bytes(yr.at[c], y_send.at[c])
-        wait_bytes(xr.at[c, 1, :, pl.ds(0, 3 * BLOCK), :], z_send.at[c])
+            wait_bytes(token_block(c, side, 0, 7), y_send.at[c, side])
+            wait_bytes(xr.at[c, 1, side, pl.ds(0, 3 * BLOCK), :], z_send.at[c, side])
 
     def e0(q):
         c, i = q // 4, q % 4
@@ -324,47 +335,38 @@
     def e_tokens(c, g, yy):
         return to_tokens(lambda e: zb2.at[c, e, g], g, yy)
 
-    def group_rows(g):
-        return rows_of(g * 2 * TOKENS, 2 * TOKENS)
-
-    def e1(c):
-        wait_bytes(zb2.at[c, pl.ds(0, 3)], z2_recv.at[c])
-
-        def body(g):
-            for side, part in enumerate(halves(e_tokens(c, g, (y + 2) % 4))):
-                ys2[c, 0, side, group_rows(g), :] = part.astype(BF)
-
-        loop(4, body)
-        y2_copy(c, 0, 0).start()
-        y2_copy(c, 0, 1).start()
-
-    def e2(c):
+    def e1(q):
+        c, g = q // 4, nth_group(q % 4)
+        at = c * 4 + g
+        wait_bytes(zb2.at[c, pl.ds(0, 3), g], z2_recv.at[c, g])
+        for side, part in enumerate(halves(e_tokens(c, g, (y + 2) % 4))):
+            ys2[at, 0, side] = part.astype(BF)
+        for side in range(2):
+            y2_copy(at, 0, side).start()
+
+    def e2(q):
+        c, g = q // 4, nth_group(q % 4)
+        at = c * 4 + g
         for side in range(2):
             other = 1 - side
-            wait_through(yr2, y2t_recv, c, other)
-
-            def body(g):
-                part = halves(e_tokens(c, g, (y + 3) % 4 if side == 0 else (y + 1) % 4))
-                rows = group_rows(g)
-                ys2[c, 1, side, rows, :] = part[side].astype(BF)
-                yr2[c, 0, other, rows, :] = (part[other] + yr2[c, 0, other, rows, :].astype(F32)).astype(BF)
-
-            loop(4, body)
-            y2_copy(c, 2, other).start()
-            y2_copy(c, 1, side).start()
-
-    def e3(c):
-        wait_tree(yr2, y2_recv, c)
-
-        def body(g):
-            rows = group_rows(g)
-            for side, part in enumerate(halves(e_tokens(c, g, y))):
-                total = part + (yr2[c, 1, side, rows, :].astype(F32) + yr2[c, 2, side, rows, :].astype(F32))
-                ye2[c, g, side] = total.astype(BF)
-
-        loop(4, body)
-        for kind in range(2):
-            for side in range(2):
+            part = halves(e_tokens(c, g, (y + 3) % 4 if side == 0 else (y + 1) % 4))
+            ys2[at, 1, side] = part[side].astype(BF)
+            wait_through(yr2, y2t_recv, at, other)
+            yr2[at, 0, other] = (part[other] + yr2[at, 0, other].astype(F32)).astype(BF)
+            y2_copy(at, 2, other).start()
+            y2_copy(at, 1, side).start()
+
+    def e3(q):
+        c, i = q // 4, q % 4
+        g = nth_group(i)
+        at = c * 4 + g
+        wait_tree(yr2, y2_recv, at)
+        for side, part in enumerate(halves(e_tokens(c, g, y))):
+            total = part + (yr2[at, 1, side].astype(F32) + yr2[at, 2, side].astype(F32))
+            ye2[c, g, side] = total.astype(BF)
+        for first, kind, side in ((0, 0, 0), (0, 0, 1), (1, 1, 0), (2, 1, 1)):
+            @pl.when(i == first)
+            def _():
                 x2_copy(c, kind, side).start()
 
     def e4(c):
@@ -378,12 +380,14 @@
         wait_tree(xr2, x2_recv, c)
         for side in range(2):
             total = ye2[c, x, side].astype(F32) + (xr2[c, 1, side].astype(F32) + xr2[c, 2, side].astype(F32))
-            fin[direct + c, :, side * HALF:(side + 1) * HALF] = total.astype(BF)
-        deliver(direct + c)
+            fin[c, :, side * HALF:(side + 1) * HALF] = total.astype(BF)
+        o_copy(c).start()
+        o_local(c).start()
 
     def e6(c):
         wait_bytes(xr2.at[c], x2_send.at[c])
-        wait_bytes(yr2.at[c], y2_send.at[c])
+        for g in range(4):
+            wait_bytes(yr2.at[c * 4 + g], y2_send.at[c * 4 + g])
 
     def old_sends(_):
         wait_bytes(a_buf.at[1], core_send.at[0])
@@ -400,25 +404,24 @@
                 wait_z2_sent(c, g)
 
     plan = (
-        (a0, (2, 3, 6, 10, 17)),
-        (functools.partial(a1, 0), (11, 19, 20, 24, 25)),
-        (functools.partial(a1, 1), (11, 19, 20, 24, 25)),
-        (e0, (0, 3, 5, 7, 8, 9, 15, 16, 17, 21, 22, 27)),
-        (share_keys, (1,)),
-        (build, (4, 9, 12, 13)),
-        (e1, (14, 23, 30)),
-        (e2, (18, 26, 33)),
-        (e3, (29, 39, 44)),
-        (e4, (38, 42, 48)),
-        (e5, (41, 49, 53)),
-        (a2, (28, 31, 34, 35, 37)),
-        (a3, (32, 34, 36, 43, 47)),
-        (a4, (35, 40, 45, 50, 52)),
-        (a5, (46, 51, 54, 55, 56)),
-        (old_sends, (32,)),
-        (last_sends, (41,)),
-        (e6, (43, 51, 55)),
-        (a6, (48, 53, 55, 56, 57)),
+        (a0, (1, 3, 5, 7, 12)),
+        (functools.partial(a1, 0), (4, 6, 17, 27, 28)),
+        (functools.partial(a1, 1), (4, 6, 17, 27, 28)),
+        (e0, (0, 1, 2, 5, 7, 8, 11, 13, 16, 19, 20, 23)),
+        (share_keys, (0,)),
+        (build, (3, 5, 7, 8)),
+        (e1, (8, 9, 10, 11, 13, 18, 22, 24, 27, 28, 31, 36)),
+        (e2, (11, 13, 14, 15, 19, 23, 25, 27, 28, 30, 34, 41)),
+        (e3, (26, 28, 29, 35, 37, 38, 39, 40, 46, 51, 52, 54)),
+        (e4, (33, 48, 52)),
+        (e5, (46, 50, 55)),
+        (a2, (19, 21, 23, 24, 29, 32, 36, 42, 44, 47)),
+        (a3, (31, 34, 38, 42, 43, 44, 45, 47, 49, 50)),
+        (a4, (36, 44, 47, 50, 51, 53, 54, 55, 56, 57)),
+        (old_sends, (37,)),
+        (last_sends, (51,)),
+        (e6, (48, 52, 57)),
+        (a5, (46, 52, 55, 57, 58)),
     )
 
     def step(n):
@@ -433,6 +436,7 @@
     mine = fin.at[:, pl.ds(0, TOKENS)]
     for i in range(3):
         wait_bytes(mine, o_sem.at[i])
+    wait_bytes(yr.at[:, :, pl.ds(0, 2)], a_sem.at[0])
 
 
 def on_device(expert_ids, hidden_grad, up_weight):
@@ -462,22 +466,21 @@
             vmem(3, 2, 2, GROUP, HALF),
             vmem(direct, 3, 2, GROUP, HALF),
             vmem(direct, 4, 2, BLOCK, HALF),
-            vmem(direct, 2, 2, both, HALF),
-            vmem(direct, 3, 2, both, HALF),
+            vmem(direct, 2, SHARDS, TOKENS, HALF),
             vmem(2, 4, 2, GROUP, HALF),
             vmem(early, 4, 4, 2, BLOCK, HALF),
-            vmem(early, 2, 2, 4 * both, HALF),
-            vmem(early, 3, 2, 4 * both, HALF),
+            vmem(early * 4, 2, 2, both, HALF),
+            vmem(early * 4, 3, 2, both, HALF),
             vmem(early, 4, 2, both, HALF),
             vmem(early, 3, 2, both, HALF),
             vmem(4, 4, both, DEPTH),
-            vmem(chunks, both, WIDE),
+            vmem(early, both, WIDE),
             pltpu.VMEM((4, SHARDS, 8, TOKENS), jnp.int32),
             dma((4 + chunks,)), dma((2,)), dma((4 + chunks,)), dma((4,)),
-            dma((direct,)), dma((direct,)), dma((direct,)), dma((direct, 2)), dma((direct,)),
-            dma((direct,)), dma((direct,)), dma((direct,)), dma((direct, 2)), dma((direct,)),
-            dma((early, 4)), dma((early,)), dma((early,)), dma((early, 2)), dma((early,)),
-            dma((early,)), dma((early, 2)), dma((early,)), dma((3,)),
+            dma((direct,)), dma((direct,)), dma((direct,)), dma((direct, 2)), dma((direct, 2)),
+            dma((direct, 2)), dma((direct, 2)), dma((direct, 2)), dma((direct, 2)),
+            dma((early, 4)), dma((early, 4)), dma((early * 4,)), dma((early * 4, 2)), dma((early * 4,)),
+            dma((early,)), dma((early, 2)), dma((early,)), dma((3,)), dma((1,)),
         ],
         compiler_params=pltpu.CompilerParams(
             collective_id=0, has_side_effects=True, vmem_limit_bytes=63 * 2**20

time: 136 us -> 130 us (0.956)
  Pallas kernels: 133 us -> 128 us
    pallas_call x1, Pallas kernels: 133 us -> 128 us  [on_device(): pl.pallas_call(functools.partial(kernel, direct, early), out_shape=jax.Sh...]
where the time goes in v3:
time: 130 us
  Pallas kernels  128 us (98%)
  local copies, waits for them, and re-layouts  2.29 us (2%)
    pallas_call x1, Pallas kernels, on_device(): pl.pallas_call(functools.partial(kernel, direct, early), out_shape=jax.Sh...  128 us

profile of v3, /device:TPU:1, one launch (start us, length us, event | category | flops | bytes accessed | tf_op | source)
XLA Modules:
  0.0 129.9 jit_solution(8525568721820366381)
XLA Ops:
  0.0 127.6 %up_cotangent.1 = bf16[128,4096]{1,0:T(8,128)(2,1)} custom-call(s32[2,128]{1,0:T(2,128)} %bitcast.5, bf16[4352,768]{1,0:T(8,128)(2,1)} %hid_ref.1, bf16[4096,768]{1,0:T(8,128)(2,1)} %w_ref.1), custom_call_target="tpu_custom_call" | custom-call | flops 27380416512 | bytes 14024704 | tf_op jit(solution)/shard_map/up_cotangent/pallas_call | solution.py:454
  127.6 2.3 %copy.5 = bf16[1,128,4096]{2,1,0:T(8,128)(2,1)} copy(bf16[1,128,4096]{2,1,0:T(8,128)(2,1)} %bitcast.4) | data formatting | bytes 2097152

commit v4 on v3

--- a/solution.py
+++ b/solution.py
@@ -453,7 +453,7 @@
 
     out = pl.pallas_call(
         functools.partial(kernel, direct, early),
-        out_shape=jax.ShapeDtypeStruct((TOKENS, width), BF),
+        out_shape=pltpu.VMEM((TOKENS, width), BF),
         in_specs=[
             pl.BlockSpec(memory_space=pltpu.VMEM),
             pl.BlockSpec(memory_space=pl.ANY),
@@ -483,7 +483,7 @@
             dma((early,)), dma((early, 2)), dma((early,)), dma((3,)), dma((1,)),
         ],
         compiler_params=pltpu.CompilerParams(
-            collective_id=0, has_side_effects=True, vmem_limit_bytes=63 * 2**20
+            collective_id=0, has_side_effects=True, vmem_limit_bytes=61 * 2**20
         ),
         cost_estimate=pl.CostEstimate(
             flops=2 * rows * hid * width, bytes_accessed=2 * (rows + width) * hid + 2 * TOKENS * width, transcendentals=0

time: 130 us -> 129 us (level)
  local copies, waits for them, and re-layouts: 2.29 us -> 0.97 us
    unnamed x1, local copies, waits for them, and re-layouts: 2.29 us -> 0.97 us
where the time goes in v4:
time: 129 us; the launch traced here: 128 us
  Pallas kernels  127 us (98%)
    pallas_call x1, Pallas kernels, on_device(): pl.pallas_call(functools.partial(kernel, direct, early), out_shape=pltpu....  127 us

profile of v4, /device:TPU:1, one launch (start us, length us, event | category | flops | bytes accessed | tf_op | source)
XLA Modules:
  0.0 128.4 jit_solution(7438689746505550142)
XLA Ops:
  0.0 127.5 %up_cotangent.1 = bf16[128,4096]{1,0:T(8,128)(2,1)S(1)} custom-call(s32[2,128]{1,0:T(2,128)} %bitcast.5, bf16[4352,768]{1,0:T(8,128)(2,1)} %hid_ref.1, bf16[4096,768]{1,0:T(8,128)(2,1)} %w_ref.1), custom_call_target="tpu_custom_call" | custom-call | flops 27380416512 | bytes 14024704 | tf_op jit(solution)/shard_map/up_cotangent/pallas_call | solution.py:454
  127.5 1.0 copy.5

commit v5 on v4

--- a/solution.py
+++ b/solution.py
@@ -94,7 +94,7 @@
         step = 1 if (side == 0) != (kind == 1) else -1
         src = recvs.at[c, 0, side] if kind == 2 else source(c, kind, side, step)
         return remote(
-            src, recvs.at[c, kind, side], s_sems[kind].at[c],
+            src, recvs.at[c, kind, side], s_sems[kind].at[c // 4 if axis == "dy" else c],
             t_sem.at[c, side] if kind == 0 else r_sem.at[c, side] if by_side else r_sem.at[c], dev(**{axis: step}),
         )
 
@@ -109,7 +109,7 @@
         dy, dk = peers[i]
         return remote(
             token_block(c, side, (y + dy) % 4 * 2 + (k + dk) % 2), yr.at[c, side, k * 4 + y],
-            y_send.at[c, side], y_recv.at[c, side], dev(dy=dy, dk=dk),
+            y_send.at[c], y_recv.at[c, side], dev(dy=dy, dk=dk),
         )
 
     y2_copy = functools.partial(
@@ -129,7 +129,7 @@
     def z_copy(c, side, dz):
         there = rows_of(((z + dz) % 4) * BLOCK, BLOCK)
         return remote(
-            xr.at[c, 1, side, there, :], zb.at[c, z, side], z_send.at[c, side], z_recv.at[c, side], dev(dz=dz)
+            xr.at[c, 1, side, there, :], zb.at[c, z, side], z_send.at[c], z_recv.at[c, side], dev(dz=dz)
         )
 
     def z2_copy(c, g, dz):
@@ -306,9 +306,8 @@
 
     def a5(c):
         wait_bytes(xr.at[c, 0], xc_send.at[c])
-        for side in range(2):
-            wait_bytes(token_block(c, side, 0, 7), y_send.at[c, side])
-            wait_bytes(xr.at[c, 1, side, pl.ds(0, 3 * BLOCK), :], z_send.at[c, side])
+        wait_bytes(xr.at[c, 2, :, pl.ds(0, 7 * TOKENS), :], y_send.at[c])
+        wait_bytes(xr.at[c, 1, :, pl.ds(0, 3 * BLOCK), :], z_send.at[c])
 
     def e0(q):
         c, i = q // 4, q % 4
@@ -386,8 +385,7 @@
 
     def e6(c):
         wait_bytes(xr2.at[c], x2_send.at[c])
-        for g in range(4):
-            wait_bytes(yr2.at[c * 4 + g], y2_send.at[c * 4 + g])
+        wait_bytes(yr2.at[pl.ds(c * 4, 4)], y2_send.at[c])
 
     def old_sends(_):
         wait_bytes(a_buf.at[1], core_send.at[0])
@@ -478,8 +476,8 @@
             pltpu.VMEM((4, SHARDS, 8, TOKENS), jnp.int32),
             dma((4 + chunks,)), dma((2,)), dma((4 + chunks,)), dma((4,)),
             dma((direct,)), dma((direct,)), dma((direct,)), dma((direct, 2)), dma((direct, 2)),
-            dma((direct, 2)), dma((direct, 2)), dma((direct, 2)), dma((direct, 2)),
-            dma((early, 4)), dma((early, 4)), dma((early * 4,)), dma((early * 4, 2)), dma((early * 4,)),
+            dma((direct,)), dma((direct, 2)), dma((direct,)), dma((direct, 2)),
+            dma((early, 4)), dma((early, 4)), dma((early,)), dma((early * 4, 2)), dma((early * 4,)),
             dma((early,)), dma((early, 2)), dma((early,)), dma((3,)), dma((1,)),
         ],
         compiler_params=pltpu.CompilerParams(

time: 129 us -> 128 us (level)
  no operation moved by 1% of the time
where the time goes in v5:
time: 128 us
  Pallas kernels  127 us (99%)
    pallas_call x1, Pallas kernels, on_device(): pl.pallas_call(functools.partial(kernel, direct, early), out_shape=pltpu....  127 us

profile of v5, /device:TPU:1, one launch (start us, length us, event | category | flops | bytes accessed | tf_op | source)
XLA Modules:
  0.0 128.3 jit_solution(630478096052405256)
XLA Ops:
  0.0 127.3 %up_cotangent.1 = bf16[128,4096]{1,0:T(8,128)(2,1)S(1)} custom-call(s32[2,128]{1,0:T(2,128)} %bitcast.5, bf16[4352,768]{1,0:T(8,128)(2,1)} %hid_ref.1, bf16[4096,768]{1,0:T(8,128)(2,1)} %w_ref.1), custom_call_target="tpu_custom_call" | custom-call | flops 27380416512 | bytes 14024704 | tf_op jit(solution)/shard_map/up_cotangent/pallas_call | solution.py:452
  127.3 1.0 copy.5
